TPU v7x, 128 devices: a whole 4x4x4 slice. The times are simulated.
128 devices in a mesh: band: 4 (over x), plane: 32 (over z, y, core).
Axes of the slice: x: 4, y: 4, z: 4, core: 2. Of those that a mesh axis runs over, the one named last changes fastest.
Arguments:
- orbitals: bfloat16 [2, 128, 13312, 128], P(None, 'band', 'plane')
- trial_bands: float32 [2, 4, 13312, 128], P(None, 'band', 'plane')
- potential: float32 [320, 320, 320], P('plane'), may hold values from -6 to 6
- stick_column: int32 [13312], P('plane'), may hold values from 0 to 16383, as said below
- stick_length: int32 [13312], P('plane'), may hold values from 0 to 127, as said below
Outputs:
- applied: float32 [2, 4, 13312, 128], P(None, 'band', 'plane')
- intersection: float32 [2, 128, 128], P(None, 'band')
- projected: float32 [2, 128, 4], P(None, 'band')
Inputs may be any that keep to these rules, and one draw needn't show every extreme that they name: stick_column holds distinct window positions; every position x * 128 + y with (x - 64)^2 + (y - 64)^2 <= 63^2 appears once, and so do positions 0 and 16383; the remaining sticks take other positions. stick_length is 2 m + 1 for the largest whole m with m^2 + ox^2 + oy^2 <= 63^2 for the stick's column offsets ox, oy, and 0 where the column lies outside that disk.
All inputs are finite; a program needn't handle non-finite values.
Results may differ from a plain program's by a relative error of at most 0.0075.
Values may be sent and summed in bfloat16 or wider, within the bound.
A program may use at most 128 MiB of HBM per device.

v0:
```python
import math

import jax
import jax.numpy as jnp
from jax import lax
from jax.sharding import PartitionSpec as P

RADIUS = 63


def sphere_masks(stick_column, stick_length, slot_count):
    centre = slot_count // 2
    slot_offsets = jnp.arange(slot_count, dtype=jnp.int32) - centre
    inside = 2 * jnp.abs(slot_offsets)[None, :] < stick_length[:, None]
    off_x = stick_column // slot_count - centre
    off_y = stick_column % slot_count - centre
    squared = (off_x * off_x + off_y * off_y)[:, None] + (slot_offsets * slot_offsets)[None, :]
    kinetic = squared.astype(jnp.float32) / jnp.float32(RADIUS * RADIUS)
    return (inside, kinetic)


def tables(slot_count, points, sign_in):
    centre = slot_count // 2
    waves = jnp.arange(slot_count, dtype=jnp.int32)[:, None] - centre
    places = jnp.arange(points, dtype=jnp.int32)[None, :]
    phases = waves * places % points
    angles = phases.astype(jnp.float32) * jnp.float32(2.0 * math.pi / points)
    return (jnp.cos(angles), sign_in * jnp.sin(angles))


def complex_apply(pattern, parts_in, table_real, table_imag):

    def real_dot(first, second):
        return jnp.einsum(pattern, first, second, precision=lax.Precision.HIGHEST)

    real_part = real_dot(parts_in[0], table_real) - real_dot(parts_in[1], table_imag)
    imag_part = real_dot(parts_in[0], table_imag) + real_dot(parts_in[1], table_real)
    return jnp.stack([real_part, imag_part])


def pair_products(left, right):

    def real_dot(first, second):
        return lax.dot_general(
            first, second, (((1, 2), (1, 2)), ((), ())), preferred_element_type=jnp.float32
        )

    real_part = real_dot(left[0], right[0]) + real_dot(left[1], right[1])
    imag_part = real_dot(left[0], right[1]) - real_dot(left[1], right[0])
    return jnp.stack([real_part, imag_part])


def shards(orbitals, trial_bands, potential, stick_column, stick_length):
    slot_count = trial_bands.shape[3]
    points = potential.shape[1]
    inside, kinetic = sphere_masks(stick_column, stick_length, slot_count)
    masked = jnp.where(inside[None, None], trial_bands, 0.0)
    inverse_real, inverse_imag = tables(slot_count, points, 1.0)
    forward_real = inverse_real.T / points
    forward_imag = -inverse_imag.T / points
    columns = lax.all_gather(stick_column, "plane", axis=0, tiled=True)
    window_ids = jnp.arange(slot_count, dtype=jnp.int32)[None, :]
    row_x = ((columns // slot_count)[:, None] == window_ids).astype(jnp.bfloat16)
    row_y = ((columns % slot_count)[:, None] == window_ids).astype(jnp.bfloat16)

    def one_plane(pair_in):
        values, field = pair_in
        spread = values[:, :, :, None] * row_y[None, None]
        window = jnp.einsum("kdsv,sa->kdav", spread, row_x, preferred_element_type=jnp.float32)
        along_y = complex_apply("dav,vy->day", window, inverse_real, inverse_imag)
        spatial = complex_apply("day,ax->dyx", along_y, inverse_real, inverse_imag)
        spatial = spatial * field[None, None]
        back_x = complex_apply("dyx,xa->dya", spatial, forward_real, forward_imag)
        back_y = complex_apply("dya,yv->dav", back_x, forward_real, forward_imag)
        back_low = back_y.astype(jnp.bfloat16)
        selected = jnp.einsum("kdav,sa->kdsv", back_low, row_x, preferred_element_type=jnp.float32)
        return jnp.sum(selected * row_y[None, None], axis=3).astype(jnp.bfloat16)

    z_values = complex_apply("bst,tz->bzs", masked, inverse_real, inverse_imag).astype(jnp.bfloat16)
    picked = lax.map(
        one_plane,
        (
            jnp.moveaxis(
                lax.all_to_all(z_values, "plane", split_axis=2, concat_axis=3, tiled=True), 2, 0
            ),
            potential,
        ),
    )
    picked = jnp.moveaxis(picked, 0, 2)
    returned = lax.all_to_all(picked, "plane", split_axis=3, concat_axis=2, tiled=True)
    local_part = complex_apply(
        "bzs,zt->bst", returned.astype(jnp.float32), forward_real, forward_imag
    )
    applied = jnp.where(inside[None, None], kinetic[None, None] * trial_bands + local_part, 0.0)
    basis = jnp.where(inside[None, None], orbitals, jnp.zeros_like(orbitals))
    applied_low = applied.astype(jnp.bfloat16)
    own_rows = orbitals.shape[1]
    basis_group, applied_group = (
        lax.all_to_all(basis, "band", split_axis=2, concat_axis=1, tiled=True),
        lax.all_to_all(applied_low, "band", split_axis=2, concat_axis=1, tiled=True),
    )
    intersection = pair_products(basis_group, basis_group)
    projected = pair_products(basis_group, applied_group)
    intersection, projected = lax.psum((intersection, projected), ("band", "plane"))
    first_row = lax.axis_index("band") * own_rows
    intersection = lax.dynamic_slice_in_dim(intersection, first_row, own_rows, 1)
    projected = lax.dynamic_slice_in_dim(projected, first_row, own_rows, 1)
    return (applied, intersection, projected)


def solution(mesh):
    return jax.shard_map(
        shards,
        mesh=mesh,
        in_specs=(
            P(None, "band", "plane", None),
            P(None, "band", "plane", None),
            P("plane", None, None),
            P("plane"),
            P("plane"),
        ),
        out_specs=(P(None, "band", "plane", None), P(None, "band", None), P(None, "band", None)),
        check_vma=False,
    )
```

profile of v0, /device:TPU:1, one launch (start us, length us, event | category | flops | bytes accessed | tf_op | source)
XLA Modules:
  0.0 899.3 jit_solution(12637198510778645193)
XLA Ops:
  16.9 9.6 %all-to-all-start = ((bf16[2,1,320,416]{3,0,1,2:T(2,128)(2,1)}), bf16[2,1,320,416]{3,0,1,2:T(2,128)(2,1)S(1)}, u32[]{:S(2)}, u32[]{:S(2)}) async-start(bf16[2,1,320,416]{3,0,1,2:T(2,128)(2,1)} %copy.64), calls=%async_computation | async-start | bytes 1310720 | tf_op jit(solution)/shard_map/all_to_all | solution.py:84
  28.1 123.3 %all-reduce = s32[13312]{0:T(1024)S(1)} all-reduce(s32[13312]{0:T(1024)S(1)} %dynamic-update-slice), channel_id=1, replica_groups=mesh['band'=4,'plane'=32] {'plane'}, use_global_device_ids=true, to_apply=%add | all-reduce | flops 13312 | bytes 106496
  152.4 336.3 %while.13 = (s32[]{:T(128)}, bf16[10,2,1,13312]{3,1,2,0:T(2,128)(2,1)S(1)}, bf16[10,2,1,13312]{3,1,2,0:T(2,128)(2,1)S(1)}, f32[10,320,320]{2,1,0:T(8,128)}, s32[...) while((s32[]{:T(128)}, ...), condition=%wide.region_2.3_spmd.clone.clone.clone, body=%wide.region_0.2_spmd.clone.clone.clone.sunk | while | flops 3535828992 | bytes 32288872 | solution.py:80
  192.0 8.2 fusion.410
  224.0 8.2 fusion.410
  256.0 8.2 fusion.410
  288.0 8.2 fusion.410
  320.0 8.2 fusion.410
  352.0 8.2 fusion.410
  384.0 8.2 fusion.410
  416.1 8.2 fusion.410
  448.1 8.2 fusion.410
  480.1 8.2 fusion.410
  488.7 10.8 %copy.67 = bf16[10,2,1,13312]{0,1,2,3:T(2,128)(2,1)} copy(bf16[10,2,1,13312]{3,1,2,0:T(2,128)(2,1)S(1)} %get-tuple-element.91) | data formatting | bytes 1064960 | tf_op jit(solution)/shard_map/while | solution.py:80
  499.5 6.8 bitcast_bitcast_fusion
  506.3 16.3 %reshape.355 = bf16[32,2,4160]{2,1,0:T(2,128)(2,1)} reshape(bf16[13312,1,2,10]{3,2,1,0:T(2,128)(2,1)} %bitcast_bitcast_fusion) | data formatting | bytes 1064960
  522.5 9.5 %all-to-all-start.1 = ((bf16[32,2,4160]{2,1,0:T(2,128)(2,1)}), bf16[32,2,4160]{2,1,0:T(2,128)(2,1)S(1)}, u32[]{:S(2)}, u32[]{:S(2)}) async-start(bf16[32,2,4160]{2,1,0:T(2,128)(2,1)} %reshape.355), calls=%async_computation.1 | async-start | bytes 1081344 | tf_op jit(solution)/shard_map/all_to_all | solution.py:90
  532.2 11.6 %all-to-all-done.1 = bf16[32,2,4160]{2,1,0:T(2,128)(2,1)S(1)} async-done(((bf16[32,2,4160]{2,1,0:T(2,128)(2,1)}), bf16[32,2,4160]{2,1,0:T(2,128)(2,1)S(1)}, u32[]{:S(2)}, u32[]{:S(2)}) %all-to-all-start.1) | async-done | bytes 532512 | tf_op jit(solution)/shard_map/all_to_all | solution.py:90
  543.8 15.4 %reshape.356 = bf16[13312,1,2,10]{3,2,1,0:T(2,128)(2,1)} reshape(bf16[32,2,4160]{2,1,0:T(2,128)(2,1)S(1)} %all-to-all-done.1) | data formatting | bytes 1064960
  559.1 11.7 %copy.81 = bf16[2,1,10,32,416]{4,3,0,2,1:T(8,128)(2,1)S(1)} copy(bf16[2,1,10,32,416]{2,0,4,3,1:T(2,128)(2,1)} %bitcast.224) | data formatting | bytes 1064960 | tf_op jit(solution)/shard_map/all_to_all | solution.py:90
  582.0 8.2 copy_select_fusion
  596.9 75.0 %all-to-all-done.2 = bf16[2,32,416,128]{3,1,0,2:T(8,128)(2,1)} async-done(((bf16[2,32,416,128]{3,1,0,2:T(8,128)(2,1)}), bf16[2,32,416,128]{3,1,0,2:T(8,128)(2,1)}, u32[]{:S(2)}, u32[]{:S(2)}) %all-to-all-start.2) | async-done | bytes 6815776 | tf_op jit(solution)/shard_map/all_to_all | solution.py:99
  685.7 64.0 %psum.15 = f32[2,128,4]{1,2,0:T(4,128)S(1)} all-reduce(f32[2,128,4]{1,2,0:T(4,128)S(1)} %pad_maximum_fusion.2), channel_id=1, replica_groups=mesh['band'=4,'plane'=32] {'band','plane'}, use_global_device_ids=true, to_apply=%region_4.5 | all-reduce | flops 1024 | bytes 8192 | tf_op jit(solution)/shard_map/psum | solution.py:104
  755.1 135.7 %all-reduce.3.cloned.1.call-done = f32[2,128,128]{2,1,0:T(8,128)} async-done(((f32[2,128,128]{2,1,0:T(8,128)}), f32[2,128,128]{2,1,0:T(8,128)}) %all-reduce.3.cloned.1.call-update) | async-done | bytes 131088 | tf_op jit(solution)/shard_map/psum | solution.py:104
  (288 shorter events, 287.0 us)
Async XLA Ops:
  10.5 16.0 %copy-start.6 = (u32[128]{0:T(128)S(1)}, u32[128]{0:T(128)}, u32[]{:S(2)}) copy-start(u32[128]{0:T(128)} %constant.106) | copy-start | bytes 1540
  10.5 17.2 %copy-start.5 = (s32[416]{0:T(512)S(1)}, s32[416]{0:T(512)}, u32[]{:S(2)}) copy-start(s32[416]{0:T(512)} %param.10) | copy-start | bytes 4996
  16.9 134.5 %all-to-all-start = ((bf16[2,1,320,416]{3,0,1,2:T(2,128)(2,1)}), bf16[2,1,320,416]{3,0,1,2:T(2,128)(2,1)S(1)}, u32[]{:S(2)}, u32[]{:S(2)}) async-start(bf16[2,1,320,416]{3,0,1,2:T(2,128)(2,1)} %copy.64), calls=%async_computation | async-start | bytes 1310720 | tf_op jit(solution)/shard_map/all_to_all | solution.py:84
  522.5 21.2 %all-to-all-start.1 = ((bf16[32,2,4160]{2,1,0:T(2,128)(2,1)}), bf16[32,2,4160]{2,1,0:T(2,128)(2,1)S(1)}, u32[]{:S(2)}, u32[]{:S(2)}) async-start(bf16[32,2,4160]{2,1,0:T(2,128)(2,1)} %reshape.355), calls=%async_computation.1 | async-start | bytes 1081344 | tf_op jit(solution)/shard_map/all_to_all | solution.py:90
  570.9 5.4 copy-start.1
  578.0 12.2 %all-to-all-start.3 = ((bf16[2,1,416,128]{3,0,1,2:T(2,128)(2,1)}), bf16[2,1,416,128]{3,0,1,2:T(2,128)(2,1)S(1)}, u32[]{:S(2)}, u32[]{:S(2)}) async-start(bf16[2,1,416,128]{3,0,1,2:T(2,128)(2,1)} %copy.73), calls=%async_computation.3 | async-start | bytes 425984 | tf_op jit(solution)/shard_map/all_to_all | solution.py:100
  590.2 81.7 %all-to-all-start.2 = ((bf16[2,32,416,128]{3,1,0,2:T(8,128)(2,1)}), bf16[2,32,416,128]{3,1,0,2:T(8,128)(2,1)}, u32[]{:S(2)}, u32[]{:S(2)}) async-start(bf16[2,32,416,128]{3,1,0,2:T(8,128)(2,1)} %copy_select_fusion), calls=%async_computation.2 | async-start | bytes 13631488 | tf_op jit(solution)/shard_map/all_to_all | solution.py:99
  595.6 295.2 %all-reduce.3.cloned.1.call-start = ((), (), s32[]{:S(2)}) async-start(), calls=%async_computation.4 | async-start | bytes 262144 | tf_op jit(solution)/shard_map/psum | solution.py:104
  678.3 6.4 copy-start
  680.0 1.7 copy-start.2
  684.7 65.0 %copy-start.4 = (f32[128,128]{1,0:T(8,128)S(1)}, f32[128,128]{1,0:T(8,128)}, u32[]{:S(2)}) copy-start(f32[128,128]{1,0:T(8,128)} %convolution_bitcast_fusion.1) | copy-start | bytes 196612
  749.6 3.0 copy-start.3
Sparse Core Ops, SparseCore 0:
  754.6 136.2 all-reduce.2
where the time goes:
time: 907 us; the launch traced here: 899 us
  matrix products  318 us (35%)
  waiting for transfers between devices  222 us (24%)
  blocking collectives  187 us (21%)
  local copies, waits for them, and re-layouts  87.4 us (10%)
  starting transfers between devices  28.7 us (3%)
  other arithmetic  22.7 us (3%)
  loops' own time  17.7 us (2%)
  between operations  15.3 us (2%)
    dot_general x168, matrix products, real_dot(): return jnp.einsum(pattern, first, second, precision=lax.Precision.HIGHEST)  204 us
    psum x1, waiting for transfers between devices, shards(): lax.psum((intersection, projected), ('band', 'plane'))  136 us
    unnamed x1, blocking collectives  123 us
    dot_general x10, matrix products, one_plane(): jnp.einsum('kdav,sa->kdsv', back_low, row_x, preferred_element_type=jnp.f...  81.6 us
    all_to_all x1, waiting for transfers between devices, shards(): lax.all_to_all(basis, 'band', split_axis=2, concat_axis=1, tiled=True)  75 us
    psum x1, blocking collectives, shards(): lax.psum((intersection, projected), ('band', 'plane'))  64 us
    unnamed x22, local copies, waits for them, and re-layouts  40 us
    dot_general x10, matrix products, one_plane(): jnp.einsum('kdsv,sa->kdav', spread, row_x, preferred_element_type=jnp.flo...  21 us
  transfers between devices with their start and end apart: 5, of which 3 were waited for; matrix products, arithmetic and copies ran while one was open for 1% of the time, Pallas kernels for 0%

commit v1 on v0

v1 whole, which is shorter than its diff:
```python
import functools
import math

import jax
import jax.numpy as jnp
import ml_dtypes
import numpy as np
from jax import lax
from jax.experimental import pallas as pl
from jax.experimental.pallas import tpu as pltpu
from jax.sharding import PartitionSpec as P

MESH = pl.DeviceIdType.MESH
BF16 = jnp.bfloat16
F32 = jnp.float32

GRID = 320
SLOT = 128
RADIUS = 63
NB = 4
NP = 32
SD = 416
ZP = GRID // NP
KZ = 2 * ZP
ROWS = 80
STICKS = NP * SD
PAD = 384
TILES = 6
EXTRA = 8 * SLOT
GROUP = 4 * SD
GROUPS = NP // 4
REDUCERS = 10


def split(table):
    table = np.asarray(table, np.float32)
    high = table.astype(ml_dtypes.bfloat16)
    low = (table - high.astype(np.float32)).astype(ml_dtypes.bfloat16)
    return high, low


@functools.lru_cache
def tables():
    half = SLOT // 2
    phase = np.outer(np.arange(SLOT) - half, np.arange(GRID)) % GRID
    cos, sin = np.cos(2 * math.pi / GRID * phase), np.sin(2 * math.pi / GRID * phase)
    full = np.zeros((NP, KZ, 2, SLOT))
    for q in range(NP):
        c, s = cos[:, q * ZP : (q + 1) * ZP].T, sin[:, q * ZP : (q + 1) * ZP].T
        full[q, :ZP, 0], full[q, :ZP, 1] = c, -s
        full[q, ZP:, 0], full[q, ZP:, 1] = s, c
    main = full[:, :16].reshape(NP * 16, 2 * SLOT)
    rest = np.tile(full[:, 16:], (1, 4, 1, 1)).reshape(NP * 16, 2 * SLOT)
    z_out = np.stack([*split(main), *split(rest)])
    z_back = np.stack([*split(main.T / GRID), *split(rest.T / GRID)])
    x_out = np.zeros((2, SLOT, 2, PAD))
    x_out[0, :, 0, :GRID], x_out[0, :, 1, :GRID] = cos, sin
    x_out[1, :, 0, :GRID], x_out[1, :, 1, :GRID] = -sin, cos
    x_out = x_out.reshape(2 * SLOT, 2 * PAD)
    y_out = np.block([[cos.T, -sin.T], [sin.T, cos.T]])
    low = ml_dtypes.bfloat16
    return dict(
        z_out=z_out,
        z_back=z_back,
        x_out=x_out.astype(low),
        y_out=y_out.astype(low),
        y_back=(y_out.T / GRID).astype(low),
        x_back=(x_out.T / GRID).astype(low),
        swap=np.eye(256).reshape(16, 16, 256).transpose(1, 0, 2).reshape(256, 256).astype(low),
    )


TABLES = ("z_out", "z_back", "x_out", "y_out", "y_back", "x_back", "swap")


def dot(first, second):
    return jnp.dot(first, second, preferred_element_type=F32)


def dot_nt(first, second):
    return lax.dot_general(first, second, (((1,), (1,)), ((), ())), preferred_element_type=F32)


def kernel(
    orbitals, trial, potential, meta, z_out_h, z_back_h, x_out_h, y_out_h, y_back_h, x_back_h, swap_h,
    applied_out, final_out,
    z_out, z_back, x_out, y_out, y_back, x_back, swap, pot,
    shares, masked, cols_out, cols_in, tx, rx, tx2, rx2,
    spots, values, onehot, spread, window, back,
    xin, yin, prod, xback, inside_s, inside_low, kinetic_s, local_s, applied, applied_low, applied_in,
    turned, turned_applied, extra_raw, extra_out, extra_in, gram, proj,
    part_out, part_in, part_sum, red_in, fin,
    load_sem, share_send, share_recv, own_sem, extra_send, extra_recv, cols_send, cols_recv, tx_send, tx_recv, tx2_send, tx2_recv,
    app_send, app_recv, part_send, part_recv, red_send, red_recv, fin_send, fin_recv, out_sem,
):
    b = lax.axis_index("band")
    p = lax.axis_index("plane")

    barrier = pltpu.get_barrier_semaphore()

    def plane_peer(i):
        return 4 * lax.rem(p // 4 + i // 4, GROUPS) + lax.rem(p + i, 4)

    def greet(i, carry):
        pl.semaphore_signal(barrier, inc=1, device_id=(b, plane_peer(i)), device_id_type=MESH)
        return carry

    lax.fori_loop(1, NP, greet, 0)
    for d in range(1, NB):
        pl.semaphore_signal(barrier, inc=1, device_id=(lax.rem(b + d, NB), p), device_id_type=MESH)

    loads = [
        pltpu.make_async_copy(source, target, load_sem.at[i])
        for i, (source, target) in enumerate(
            [
                (z_out_h, z_out), (z_back_h, z_back), (x_out_h, x_out), (y_out_h, y_out), (y_back_h, y_back),
                (x_back_h, x_back), (swap_h, swap), (potential, pot),
                (orbitals.at[:, :, pl.ds(16 * 4 * TILES, 32), :], extra_raw),
            ]
        )
    ]
    for load in loads:
        load.start()

    shift = 32 * lax.rem(p, 4)
    rest = 384 + pl.multiple_of(shift, 32)
    cols_out[0:3, :] = meta[0:3, :]
    cols_out[3:4, :] = pltpu.roll(meta[0:8, :], shift, 1)[3:4, :]
    cols_out[4:8, :] = jnp.zeros((4, SLOT), jnp.int32)
    slots = lax.broadcasted_iota(jnp.int32, (SLOT, SLOT), 1) - SLOT // 2
    for t in range(4):
        rows = SLOT if t < 3 else SD - 3 * SLOT
        as_column = jnp.broadcast_to(meta[t : t + 1, :].astype(F32), (SLOT, SLOT)).T.astype(jnp.int32)
        length = jnp.broadcast_to(meta[4 + t : 5 + t, :].astype(F32), (SLOT, SLOT)).T.astype(jnp.int32)
        inside = (2 * jnp.abs(slots) < length).astype(F32)
        off_x, off_y = (as_column >> 7) - SLOT // 2, (as_column & 127) - SLOT // 2
        squared = off_x * off_x + off_y * off_y + slots * slots
        kinetic = squared.astype(F32) / F32(RADIUS * RADIUS)
        where = pl.ds(t * SLOT, rows)
        inside_s[where, :] = inside[:rows]
        kinetic_s[where, :] = kinetic[:rows]
    inside_low[...] = inside_s[...].astype(BF16)

    for k in range(2):
        masked[k, 384:512, :] = jnp.zeros((SLOT, SLOT), F32)
        masked[k, 0:384, :] = trial[k, 0, 0:384, :] * inside_s[0:384, :]
        masked[k, pl.ds(rest, 32), :] = trial[k, 0, 384:SD, :] * inside_s[384:SD, :]
    turned_trial = jnp.concatenate([masked[0].T, masked[1].T], axis=0)
    high = turned_trial.astype(BF16)
    low = (turned_trial - high.astype(F32)).astype(BF16)
    loads[0].wait()

    def z_dot(i):
        return dot(z_out[i], high) + (dot(z_out[i + 1], high) + dot(z_out[i], low))

    main = z_dot(0)
    for t in range(4):
        tx[:, 16 * t : 16 * t + 16, :] = main[:, t * SLOT : (t + 1) * SLOT].reshape(NP, 16, SLOT).astype(BF16)
    every = z_dot(2)
    quarter = (lax.broadcasted_iota(jnp.int32, (NP * 16, SLOT), 0) >> 2) & 3
    tail = jnp.zeros((NP * 16, SLOT), F32)
    for t in range(4):
        tail = jnp.where(quarter == t, every[:, t * SLOT : (t + 1) * SLOT], tail)
    tx[:, 64:80, :] = tail.reshape(NP, 16, SLOT).astype(BF16)

    def block_copy(q, source, out_ref, in_ref, send, recv):
        return pltpu.make_async_remote_copy(
            src_ref=out_ref.at[q], dst_ref=in_ref.at[source], send_sem=send, recv_sem=recv,
            device_id=(b, q), device_id_type=MESH,
        )

    def all_copies(out_ref, in_ref, send, recv, first=0, count=NP - 1):
        where = pl.ds(first, count)
        return pltpu.make_async_remote_copy(
            src_ref=out_ref.at[where], dst_ref=in_ref.at[where], send_sem=send, recv_sem=recv,
            device_id=(b, lax.rem(p + 1, NP)), device_id_type=MESH,
        )

    pl.semaphore_wait(barrier, NP - 1 + NB - 1)

    def share_rows(c, j):
        return pl.ds(pl.multiple_of((TILES * c + j) * 16, 16), 16)

    def share_copy(c, j, source):
        return pltpu.make_async_remote_copy(
            src_ref=orbitals.at[:, :, share_rows(c, j), :], dst_ref=shares.at[source, j],
            send_sem=share_send.at[c, j], recv_sem=share_recv.at[source, j],
            device_id=(c, p), device_id_type=MESH,
        )

    def own_copy(j):
        return pltpu.make_async_copy(orbitals.at[:, :, share_rows(b, j), :], shares.at[b, j], own_sem.at[j])

    def send_shares(j, carry):
        for d in range(1, NB):
            share_copy(lax.rem(b + d, NB), j, b).start()
        own_copy(j).start()
        return carry

    send_shares(0, 0)

    def cols_copy(q, source):
        return pltpu.make_async_remote_copy(
            src_ref=cols_out, dst_ref=cols_in.at[source], send_sem=cols_send, recv_sem=cols_recv,
            device_id=(b, q), device_id_type=MESH,
        )

    def send_cols(i, carry):
        cols_copy(plane_peer(i), p).start()
        return carry

    lax.fori_loop(1, NP, send_cols, 0)

    def send_tx(i, carry):
        block_copy(plane_peer(i), p, tx, rx, tx_send, tx_recv.at[p // 4]).start()
        return carry

    lax.fori_loop(1, NP, send_tx, 0)
    cols_in[p] = cols_out[...]
    rx[p] = tx[p]

    lax.fori_loop(1, TILES, send_shares, 0)

    gram[...] = jnp.zeros_like(gram)
    proj[...] = jnp.zeros_like(proj)

    def gram_step(j):
        own_copy(j).wait()
        for d in range(1, NB):
            c = lax.rem(b + d, NB)
            share_copy(c, j, c).wait_recv()
        mask = inside_low[share_rows(b, j), :]
        for k in range(2):
            for c in range(NB):
                halves = [
                    (shares[c, j, k, half * 16 : (half + 1) * 16] * mask[None]).reshape(256, SLOT) for half in range(2)
                ]
                flipped = dot(swap[...], jnp.concatenate(halves, axis=1)).astype(BF16)
                for half in range(2):
                    row = k * 128 + c * 32 + half * 16
                    for i in range(16):
                        lane = j * 2048 + i * SLOT
                        turned[row : row + 16, lane : lane + SLOT] = flipped[
                            i * 16 : i * 16 + 16, half * SLOT : (half + 1) * SLOT
                        ]
        block = turned[:, j * 2048 : (j + 1) * 2048]
        gram[...] += dot_nt(block, block)

    all_copies(cols_in, cols_in, cols_send, cols_recv).wait_recv()

    def group_lanes(g):
        return pl.ds(pl.multiple_of(g * GROUP, SLOT), GROUP)

    def fill_onehot(g, carry):
        where = group_lanes(g)
        pieces = [cols_in[4 * g + r, t : t + 1, :] for r in range(4) for t in range(3)]
        pieces.append(sum(cols_in[4 * g + r, 3:4, :] for r in range(1, 4)) + cols_in[4 * g, 3:4, :])
        group_cols = jnp.concatenate(pieces, axis=1)
        col_y = group_cols & 127
        spot = ((col_y >> 5) << 7) + (group_cols >> 7)
        spots[0:1, where] = col_y & 31
        for r in range(4):
            ids = lax.broadcasted_iota(jnp.int32, (SLOT, GROUP), 0) + r * SLOT
            onehot[r * SLOT : (r + 1) * SLOT, where] = (ids == spot).astype(F32).astype(BF16)
        return carry

    lax.fori_loop(0, GROUPS, fill_onehot, 0)

    window[...] = jnp.zeros_like(window)

    def to_window(i, carry):
        g = lax.rem(p // 4 + GROUPS - i, GROUPS)
        where = group_lanes(g)

        @pl.when(i == 0)
        def _():
            all_copies(tx, rx, tx_send, tx_recv.at[g], 0, 3).wait_recv()

        @pl.when(i > 0)
        def _():
            all_copies(tx, rx, tx_send, tx_recv.at[g], 0, 4).wait_recv()

        rest_block = jnp.zeros((32, SLOT), F32)
        for r in range(4):
            block = rx[4 * g + r].astype(F32)
            for t in range(3):
                lane = (3 * r + t) * SLOT
                values[0:16, lane : lane + SLOT] = block[16 * t : 16 * t + 16]
                values[16:20, lane : lane + SLOT] = block[64 + 4 * t : 68 + 4 * t]
            rest_block = rest_block + block[48:80]
        values[0:16, 12 * SLOT : GROUP] = rest_block[0:16]
        values[16:20, 12 * SLOT : GROUP] = rest_block[28:32]
        here = lax.broadcasted_iota(jnp.int32, (32, GROUP), 0) == spots[0:1, where]
        for r in range(KZ):
            spread[r * 32 : (r + 1) * 32, :] = jnp.where(here, values[r : r + 1, :], 0.0).astype(BF16)
        window[...] += dot_nt(spread[...], onehot[:, where])
        return carry

    lax.fori_loop(0, GROUPS, to_window, 0)

    loads[6].wait()
    loads[8].wait()
    for t in range(2):
        mask = inside_low[384 + 16 * t : 400 + 16 * t, :]
        for k in range(2):
            halves = [
                (extra_raw[k, half * 16 : (half + 1) * 16, 16 * t : 16 * t + 16] * mask[None]).reshape(256, SLOT)
                for half in range(2)
            ]
            flipped = dot(swap[...], jnp.concatenate(halves, axis=1)).astype(BF16)
            for half in range(2):
                for i in range(16):
                    lane = (16 * t + i) * SLOT
                    extra_out[k, half * 16 : half * 16 + 16, lane : lane + SLOT] = flipped[
                        i * 16 : i * 16 + 16, half * SLOT : (half + 1) * SLOT
                    ]

    def extra_copy(c, source):
        return pltpu.make_async_remote_copy(
            src_ref=extra_out.at[:, :, pl.ds(pl.multiple_of(c * EXTRA, EXTRA), EXTRA)], dst_ref=extra_in.at[source],
            send_sem=extra_send.at[c], recv_sem=extra_recv.at[source], device_id=(c, p), device_id_type=MESH,
        )

    gram_step(0)

    for load in loads[2:6]:
        load.wait()
    loads[7].wait()
    prod[...] = jnp.zeros_like(prod)

    def planes(i, carry):
        for h in range(2):
            z = 2 * i + h
            for k in range(2):
                for v in range(4):
                    piece = window[pl.ds(pl.multiple_of((k * ZP + z) * 32, 32), 32), v * SLOT : (v + 1) * SLOT]
                    rows = h * SLOT + v * 32
                    xin[rows : rows + 32, k * SLOT : (k + 1) * SLOT] = piece.astype(BF16)
        along_x = dot(xin[...], x_out[...])
        for h in range(2):
            for k in range(2):
                piece = along_x[h * SLOT : (h + 1) * SLOT, k * PAD : (k + 1) * PAD]
                yin[k * SLOT : (k + 1) * SLOT, h * PAD : (h + 1) * PAD] = piece.astype(BF16)
        spatial = dot(y_out[...], yin[...])
        for h in range(2):
            field = pot[2 * i + h]
            for k in range(2):
                piece = spatial[k * GRID : (k + 1) * GRID, h * PAD : h * PAD + GRID]
                prod[k * GRID : (k + 1) * GRID, h * PAD : h * PAD + GRID] = (piece * field).astype(BF16)
        back_y = dot(y_back[...], prod[...])
        for h in range(2):
            for k in range(2):
                piece = back_y[k * SLOT : (k + 1) * SLOT, h * PAD : (h + 1) * PAD]
                xback[h * SLOT : (h + 1) * SLOT, k * PAD : (k + 1) * PAD] = piece.astype(BF16)
        back_x = dot(xback[...], x_back[...])
        for h in range(2):
            z = 2 * i + h
            for k in range(2):
                for v in range(4):
                    rows = h * SLOT + v * 32
                    piece = back_x[rows : rows + 32, k * SLOT : (k + 1) * SLOT]
                    where = pl.ds(pl.multiple_of((k * ZP + z) * 32, 32), 32)
                    back[where, v * SLOT : (v + 1) * SLOT] = piece.astype(BF16)
        return carry

    lax.fori_loop(0, ZP // 2, planes, 0)

    gram_step(1)

    def from_window(i, carry):
        g = lax.rem(p // 4 + 1 + i, GROUPS)
        where = group_lanes(g)
        here = lax.broadcasted_iota(jnp.int32, (32, GROUP), 0) == spots[0:1, where]
        found = dot(back[...], onehot[:, where])
        for r in range(KZ):
            picked = jnp.where(here, found[r * 32 : (r + 1) * 32], 0.0)
            values[r : r + 1, :] = jnp.sum(picked, axis=0, keepdims=True)
        for r in range(4):
            q = 4 * g + r
            lanes = [slice((3 * r + t) * SLOT, (3 * r + t + 1) * SLOT) for t in range(3)] + [slice(12 * SLOT, GROUP)]
            for t in range(4):
                tx2[q, 16 * t : 16 * t + 16, :] = values[0:16, lanes[t]].astype(BF16)
            tx2[q, 64:80, :] = jnp.concatenate([values[16:20, lane] for lane in lanes], axis=0).astype(BF16)

        def send_back(r, carry):
            q = 4 * g + r

            @pl.when(q != p)
            def _():
                block_copy(q, p, tx2, rx2, tx2_send, tx2_recv).start()

            return carry

        lax.fori_loop(0, 4, send_back, 0)
        return carry

    lax.fori_loop(0, GROUPS, from_window, 0)
    rx2[p] = tx2[p]
    gram_step(2)

    all_copies(tx2, rx2, tx2_send, tx2_recv).wait_recv()

    loads[1].wait()
    rest_low = rx2[:, 64:80, :].reshape(NP * 16, SLOT).astype(F32)
    for t in range(4):
        first = rx2[:, 16 * t : 16 * t + 16, :].reshape(NP * 16, SLOT)
        second = jnp.where(quarter == t, rest_low, 0.0).astype(BF16)
        turned_local = (dot(z_back[0], first) + dot(z_back[2], second)) + (
            dot(z_back[1], first) + dot(z_back[3], second)
        )
        for k in range(2):
            local_s[k, t * SLOT : (t + 1) * SLOT, :] = turned_local[k * SLOT : (k + 1) * SLOT].T
    for k in range(2):
        for where, source in ((slice(0, 384), slice(0, 384)), (slice(384, SD), pl.ds(rest, 32))):
            kept = inside_s[where, :] * (kinetic_s[where, :] * trial[k, 0, where, :] + local_s[k, source, :])
            applied[k, 0, where, :] = kept
            applied_low[k, where, :] = kept.astype(BF16)
    applied_write = pltpu.make_async_copy(applied, applied_out, out_sem)
    applied_write.start()

    def app_rows(c, j):
        if j < TILES:
            return share_rows(c, j)
        return pl.ds(pl.multiple_of((4 * TILES + c // 2) * 16, 16), 16)

    def app_copy(c, j, source):
        return pltpu.make_async_remote_copy(
            src_ref=applied_low.at[:, app_rows(c, j), :], dst_ref=applied_in.at[j, source],
            send_sem=app_send.at[c, j], recv_sem=app_recv.at[source, j],
            device_id=(c, p), device_id_type=MESH,
        )

    for j in range(TILES + 1):
        for d in range(1, NB):
            app_copy(lax.rem(b + d, NB), j, b).start()
        applied_in[j, b] = applied_low[:, app_rows(b, j), :]
    for d in range(1, NB):
        extra_copy(lax.rem(b + d, NB), b).start()
    extra_in[b] = extra_out[:, :, pl.ds(pl.multiple_of(b * EXTRA, EXTRA), EXTRA)]
    gram_step(3)
    gram_step(4)

    def applied_rows(j):
        for d in range(1, NB):
            c = lax.rem(b + d, NB)
            app_copy(c, j, c).wait_recv()
        empty = jnp.zeros((4, 16, SLOT), BF16)
        pieces = [applied_in[j, c, k][None] for k in range(2) for c in range(NB)]
        gathered = jnp.concatenate(pieces[:4] + [empty] + pieces[4:] + [empty], axis=0).reshape(256, SLOT)
        flipped = dot(swap[...], gathered).astype(BF16)
        for i in range(16):
            turned_applied[:, i * SLOT : (i + 1) * SLOT] = flipped[i * 16 : i * 16 + 16]

    def applied_step(j):
        applied_rows(j)
        proj[...] += dot_nt(turned_applied[...], turned[:, j * 2048 : (j + 1) * 2048])

    for j in range(5):
        applied_step(j)
    gram_step(5)
    applied_step(5)
    for d in range(1, NB):
        c = lax.rem(b + d, NB)
        extra_copy(c, c).wait_recv()
    extra = jnp.concatenate([extra_in[c, k] for k in range(2) for c in range(NB)], axis=0)
    gram[...] += dot_nt(extra, extra)
    applied_rows(TILES)
    half = pl.ds(pl.multiple_of(lax.rem(b, 2) * EXTRA, EXTRA), EXTRA)
    proj[...] += dot_nt(turned_applied[:, half], extra)

    real = gram[0:128, 0:128] + gram[128:256, 128:256]
    imag = gram[0:128, 128:256] - gram[128:256, 0:128]
    proj_real = proj[0:8, 0:128] + proj[8:16, 128:256]
    proj_imag = proj[8:16, 0:128] - proj[0:8, 128:256]
    for c in range(NB):
        part_out[c, 0:32, :] = real[c * 32 : (c + 1) * 32]
        part_out[c, 32:64, :] = imag[c * 32 : (c + 1) * 32]
        part_out[c, 64:72, :] = proj_real
        part_out[c, 72:80, :] = proj_imag

    def part_copy(c, source):
        return pltpu.make_async_remote_copy(
            src_ref=part_out.at[c], dst_ref=part_in.at[source], send_sem=part_send.at[c], recv_sem=part_recv.at[source],
            device_id=(c, p), device_id_type=MESH,
        )

    for d in range(1, NB):
        part_copy(lax.rem(b + d, NB), b).start()
    part_in[b] = part_out[b]
    for d in range(1, NB):
        c = lax.rem(b + d, NB)
        part_copy(c, c).wait_recv()
    part_sum[...] = ((part_in[0] + part_in[1]) + (part_in[2] + part_in[3])).reshape(REDUCERS, 8, SLOT)

    def red_copy(t):
        return pltpu.make_async_remote_copy(
            src_ref=part_sum.at[t], dst_ref=red_in.at[p], send_sem=red_send.at[t], recv_sem=red_recv,
            device_id=(b, 3 * t), device_id_type=MESH,
        )

    def fin_copy(t, q):
        return pltpu.make_async_remote_copy(
            src_ref=fin.at[t], dst_ref=fin.at[t], send_sem=fin_send, recv_sem=fin_recv.at[t],
            device_id=(b, q), device_id_type=MESH,
        )

    mine = p // 3
    reducer = jnp.logical_and(lax.rem(p, 3) == 0, mine < REDUCERS)

    def send_red(t, carry):
        @pl.when(3 * t != p)
        def _():
            red_copy(t).start()

        return carry

    lax.fori_loop(0, REDUCERS, send_red, 0)

    @pl.when(reducer)
    def _():
        red_in[p] = part_sum[mine]
        all_copies(red_in, red_in, fin_send, red_recv).wait_recv()
        fin[mine] = jnp.sum(red_in[...], axis=0)

        def send_fin(i, carry):
            fin_copy(mine, plane_peer(i)).start()
            return carry

        lax.fori_loop(1, NP, send_fin, 0)

    def wait_fin(t, carry):
        @pl.when(3 * t != p)
        def _():
            fin_copy(t, 3 * t).wait_recv()

        return carry

    lax.fori_loop(0, REDUCERS, wait_fin, 0)
    final_out[...] = fin[...]

    all_copies(cols_in, cols_in, cols_send, cols_recv).wait_send()
    all_copies(tx, rx, tx_send, tx_recv.at[0]).wait_send()
    all_copies(tx2, rx2, tx2_send, tx2_recv).wait_send()

    @pl.when(reducer)
    def _():
        all_copies(red_in, red_in, fin_send, red_recv).wait_send()

    def red_sent(t, carry):
        @pl.when(3 * t != p)
        def _():
            red_copy(t).wait_send()

        return carry

    lax.fori_loop(0, REDUCERS, red_sent, 0)
    for d in range(1, NB):
        c = lax.rem(b + d, NB)
        extra_copy(c, b).wait_send()
        part_copy(c, b).wait_send()
        for j in range(TILES):
            share_copy(c, j, b).wait_send()
        for j in range(TILES + 1):
            app_copy(c, j, b).wait_send()
    applied_write.wait()


def finish(applied, final, applied_out, intersection, projected):
    applied_out[...] = applied[...]
    shift = lax.rem(SLOT - lax.axis_index("band") * 32, SLOT)
    for k in range(2):
        for r in range(4):
            intersection[k, 8 * r : 8 * r + 8, :] = final[4 * k + r]
        projected[k] = pltpu.roll(final[8 + k], shift, 1)[0:NB, 0:32]


def shards(orbitals, trial_bands, potential, stick_column, stick_length):
    pad = (0, 4 * SLOT - SD)
    meta = jnp.concatenate([jnp.pad(stick_column, pad), jnp.pad(stick_length, pad)]).reshape(8, SLOT)
    held = tables()
    any_spec = pl.BlockSpec(memory_space=pl.ANY)
    vmem_spec = pl.BlockSpec(memory_space=pltpu.VMEM)
    vmem = pltpu.VMEM
    sem = pltpu.SemaphoreType.DMA
    applied, final = pl.pallas_call(
        kernel,
        out_shape=(
            jax.ShapeDtypeStruct(trial_bands.shape, F32),
            jax.ShapeDtypeStruct((REDUCERS, 8, SLOT), F32),
        ),
        in_specs=[any_spec, vmem_spec, any_spec, vmem_spec] + [any_spec] * len(TABLES),
        out_specs=(any_spec, vmem_spec),
        scratch_shapes=[vmem(held[name].shape, BF16) for name in TABLES]
        + [
            vmem((ZP, GRID, GRID), F32),
            vmem((NB, TILES, 2, 32, 16, SLOT), BF16),
            vmem((2, 512, SLOT), F32),
            vmem((8, SLOT), jnp.int32),
            vmem((NP, 8, SLOT), jnp.int32),
            vmem((NP, ROWS, SLOT), BF16),
            vmem((NP, ROWS, SLOT), BF16),
            vmem((NP, ROWS, SLOT), BF16),
            vmem((NP, ROWS, SLOT), BF16),
            vmem((8, STICKS), jnp.int32),
            vmem((24, GROUP), F32),
            vmem((4 * SLOT, STICKS), BF16),
            vmem((KZ * 32, GROUP), BF16),
            vmem((KZ * 32, 4 * SLOT), F32),
            vmem((KZ * 32, 4 * SLOT), BF16),
            vmem((2 * SLOT, 2 * SLOT), BF16),
            vmem((2 * SLOT, 2 * PAD), BF16),
            vmem((2 * GRID, 2 * PAD), BF16),
            vmem((2 * SLOT, 2 * PAD), BF16),
            vmem((SD, SLOT), F32),
            vmem((SD, SLOT), BF16),
            vmem((SD, SLOT), F32),
            vmem((2, 512, SLOT), F32),
            vmem((2, 1, SD, SLOT), F32),
            vmem((2, SD, SLOT), BF16),
            vmem((TILES + 1, NB, 2, 16, SLOT), BF16),
            vmem((256, TILES * 2048), BF16),
            vmem((16, 2048), BF16),
            vmem((2, 32, 32, SLOT), BF16),
            vmem((2, 32, 32 * SLOT), BF16),
            vmem((NB, 2, 32, EXTRA), BF16),
            vmem((256, 256), F32),
            vmem((16, 256), F32),
            vmem((NB, 80, SLOT), F32),
            vmem((NB, 80, SLOT), F32),
            vmem((REDUCERS, 8, SLOT), F32),
            vmem((NP, 8, SLOT), F32),
            vmem((REDUCERS, 8, SLOT), F32),
            sem((9,)),
            sem((NB, TILES)),
            sem((NB, TILES)),
            sem((TILES,)),
            sem((NB,)),
            sem((NB,)),
            sem,
            sem,
            sem,
            sem((GROUPS,)),
            sem,
            sem,
            sem((NB, TILES + 1)),
            sem((NB, TILES + 1)),
            sem((NB,)),
            sem((NB,)),
            sem((REDUCERS,)),
            sem,
            sem,
            sem((REDUCERS,)),
            sem,
        ],
        compiler_params=pltpu.CompilerParams(
            collective_id=0, has_side_effects=True, vmem_limit_bytes=62 * 1024 * 1024
        ),
    )(orbitals, trial_bands, potential, meta, *[jnp.asarray(held[name]) for name in TABLES])
    applied, intersection, projected = pl.pallas_call(
        finish,
        out_shape=(
            jax.ShapeDtypeStruct(trial_bands.shape, F32),
            jax.ShapeDtypeStruct((2, 32, SLOT), F32),
            jax.ShapeDtypeStruct((2, NB, 32), F32),
        ),
        in_specs=[vmem_spec, vmem_spec],
        out_specs=(vmem_spec, vmem_spec, vmem_spec),
    )(applied, final)
    return applied, intersection, jnp.swapaxes(projected, 1, 2)


def solution(mesh):
    return jax.shard_map(
        shards,
        mesh=mesh,
        in_specs=(
            P(None, "band", "plane", None),
            P(None, "band", "plane", None),
            P("plane", None, None),
            P("plane"),
            P("plane"),
        ),
        out_specs=(P(None, "band", "plane", None), P(None, "band", None), P(None, "band", None)),
        check_vma=False,
    )
```

time: 907 us -> 108 us (0.12)
  matrix products: 318 us -> 0 us
  waiting for transfers between devices: 222 us -> 0 us
  blocking collectives: 187 us -> 0 us
  Pallas kernels: 0 us -> 106 us
  local copies, waits for them, and re-layouts: 87.4 us -> 0.7 us
  starting transfers between devices: 28.7 us -> 0 us
  other arithmetic: 22.7 us -> 0.6 us
  loops' own time: 17.7 us -> 0 us
  between operations: 15.3 us -> 0.64 us
    dot_general x196 -> x0, matrix products: 318 us -> none  [the longest x168 204 us: real_dot(): return jnp.einsum(pattern, first, second, precision=lax.Precision.HIGHEST)]
    psum x1 -> x0, waiting for transfers between devices: 136 us -> none  [shards(): lax.psum((intersection, projected), ('band', 'plane'))]
    unnamed x1 -> x0, blocking collectives: 123 us -> none
    pallas_call x0 -> x2, Pallas kernels: none -> 106 us  [the longest x1 104 us: shards(): pl.pallas_call(kernel, out_shape=(jax.ShapeDtypeStruct(trial_bands.shape,...]
    all_to_all x4 -> x0, waiting for transfers between devices: 86.6 us -> none  [the longest x1 75 us: shards(): lax.all_to_all(basis, 'band', split_axis=2, concat_axis=1, tiled=True)]
    psum x1 -> x0, blocking collectives: 64 us -> none  [shards(): lax.psum((intersection, projected), ('band', 'plane'))]
    unnamed x22 -> x0, local copies, waits for them, and re-layouts: 40 us -> none
    all_to_all x4 -> x0, starting transfers between devices: 28.5 us -> none  [the longest x1 9.6 us: shards(): lax.all_to_all(z_values, 'plane', split_axis=2, concat_axis=3, tiled=True)]
  transfers between devices with their start and end apart: 5 -> 0, of which waited for: 3 -> 0; matrix products, arithmetic and copies ran while one was open for 1% -> 0% of each run, Pallas kernels for 0% -> 0%
where the time goes in v1:
time: 108 us
  Pallas kernels  106 us (98%)
    pallas_call x1, Pallas kernels, shards(): pl.pallas_call(kernel, out_shape=(jax.ShapeDtypeStruct(trial_bands.shape,...  104 us

profile of v1, /device:TPU:1, one launch (start us, length us, event | category | flops | bytes accessed | tf_op | source)
XLA Modules:
  0.0 107.7 jit_solution(4305084409558852033)
XLA Ops:
  0.6 0.7 pad_bitcast_fusion
  1.3 0.6 pad_add_fusion.meta
  1.9 104.0 %shard_map.139 = (f32[2,1,416,128]{3,2,1,0:T(8,128)}, f32[10,8,128]{2,1,0:T(8,128)}) custom-call(bf16[2,32,416,128]{3,2,1,0:T(8,128)(2,1)} %orbitals.1, f32[2,1,416,128]{3,2,1,0:T(8,128)} %trial.1, f32[10,320,320]{2,1,0:T(8,128)} %potential.1, s32[8,128]{1,0:T(8,128)} %pad_add_fusion.meta, bf16[4,512,256]{2,1,0:T(8,128)(2,1)} %constant.16.clone.z_out_h, ...), custom_call_target="tpu_custom_call" | custom-call | tf_op jit(solution)/shard_map/pallas_call | solution.py:585
  105.9 1.8 %shard_map.140 = (f32[2,1,416,128]{3,2,1,0:T(8,128)}, f32[2,32,128]{2,1,0:T(8,128)}, f32[2,4,32]{2,1,0:T(4,128)}) custom-call(f32[2,1,416,128]{3,2,1,0:T(8,128)} %get-tuple-element.8.applied, f32[10,8,128]{2,1,0:T(8,128)} %get-tuple-element.9.final), custom_call_target="tpu_custom_call" | custom-call | tf_op jit(solution)/shard_map/pallas_call | solution.py:659

commit v2 on v1

--- a/solution.py
+++ b/solution.py
@@ -82,16 +82,16 @@
 
 
 def kernel(
-    orbitals, trial, potential, meta, z_out_h, z_back_h, x_out_h, y_out_h, y_back_h, x_back_h, swap_h,
+    orbitals, trial_h, potential, columns_h, lengths_h, z_out_h, z_back_h, x_out_h, y_out_h, y_back_h, x_back_h, swap_h,
     applied_out, final_out,
-    z_out, z_back, x_out, y_out, y_back, x_back, swap, pot,
+    z_out, z_back, x_out, y_out, y_back, x_back, swap, pot, trial, columns, lengths,
     shares, masked, cols_out, cols_in, tx, rx, tx2, rx2,
     spots, values, onehot, spread, window, back,
     xin, yin, prod, xback, inside_s, inside_low, kinetic_s, local_s, applied, applied_low, applied_in,
     turned, turned_applied, extra_raw, extra_out, extra_in, gram, proj,
     part_out, part_in, part_sum, red_in, fin,
     load_sem, share_send, share_recv, own_sem, extra_send, extra_recv, cols_send, cols_recv, tx_send, tx_recv, tx2_send, tx2_recv,
-    app_send, app_recv, part_send, part_recv, red_send, red_recv, fin_send, fin_recv, out_sem,
+    app_send, app_recv, part_send, part_recv, red_send, red_recv, fin_send, fin_recv, out_sem, joined,
 ):
     b = lax.axis_index("band")
     p = lax.axis_index("plane")
@@ -101,16 +101,57 @@
     def plane_peer(i):
         return 4 * lax.rem(p // 4 + i // 4, GROUPS) + lax.rem(p + i, 4)
 
-    def greet(i, carry):
-        pl.semaphore_signal(barrier, inc=1, device_id=(b, plane_peer(i)), device_id_type=MESH)
-        return carry
-
-    lax.fori_loop(1, NP, greet, 0)
+    row, seat = p // 8, lax.rem(p, 8)
+
+    def row_peer(i):
+        return 8 * row + lax.rem(seat + i, 8)
+
     for d in range(1, NB):
         pl.semaphore_signal(barrier, inc=1, device_id=(lax.rem(b + d, NB), p), device_id_type=MESH)
-
+        pl.semaphore_signal(barrier, inc=1, device_id=(b, 8 * lax.rem(row + d, 4) + seat), device_id_type=MESH)
+
+    def greet(i, carry):
+        pl.semaphore_signal(barrier, inc=1, device_id=(b, row_peer(i)), device_id_type=MESH)
+        return carry
+
+    lax.fori_loop(1, 8, greet, 0)
     loads = [
         pltpu.make_async_copy(source, target, load_sem.at[i])
+        for i, (source, target) in enumerate([(columns_h, columns), (lengths_h, lengths), (trial_h, trial)])
+    ]
+    for load in loads:
+        load.start()
+    pl.semaphore_wait(barrier, 3 + 3 + 7)
+
+    def tell(i, carry):
+        pl.semaphore_signal(joined, inc=1, device_id=(b, row_peer(i)), device_id_type=MESH)
+        return carry
+
+    lax.fori_loop(1, 8, tell, 0)
+
+    def share_rows(c, j):
+        return pl.ds(pl.multiple_of((TILES * c + j) * 16, 16), 16)
+
+    def share_copy(c, j, source):
+        return pltpu.make_async_remote_copy(
+            src_ref=orbitals.at[:, :, share_rows(c, j), :], dst_ref=shares.at[source, j],
+            send_sem=share_send.at[c, j], recv_sem=share_recv.at[source, j],
+            device_id=(c, p), device_id_type=MESH,
+        )
+
+    def own_copy(j):
+        return pltpu.make_async_copy(orbitals.at[:, :, share_rows(b, j), :], shares.at[b, j], own_sem.at[j])
+
+    def send_shares(j, carry):
+        for d in range(1, NB):
+            share_copy(lax.rem(b + d, NB), j, b).start()
+        own_copy(j).start()
+        return carry
+
+    lax.fori_loop(0, TILES, send_shares, 0)
+
+    loads += [
+        pltpu.make_async_copy(source, target, load_sem.at[3 + i])
         for i, (source, target) in enumerate(
             [
                 (z_out_h, z_out), (z_back_h, z_back), (x_out_h, x_out), (y_out_h, y_out), (y_back_h, y_back),
@@ -119,19 +160,21 @@
             ]
         )
     ]
-    for load in loads:
+    for load in loads[3:]:
         load.start()
+    for load in loads[:3]:
+        load.wait()
 
     shift = 32 * lax.rem(p, 4)
     rest = 384 + pl.multiple_of(shift, 32)
-    cols_out[0:3, :] = meta[0:3, :]
-    cols_out[3:4, :] = pltpu.roll(meta[0:8, :], shift, 1)[3:4, :]
+    cols_out[0:4, :] = columns[...]
     cols_out[4:8, :] = jnp.zeros((4, SLOT), jnp.int32)
+    cols_out[3:4, :] = pltpu.roll(cols_out[...], shift, 1)[3:4, :]
     slots = lax.broadcasted_iota(jnp.int32, (SLOT, SLOT), 1) - SLOT // 2
     for t in range(4):
         rows = SLOT if t < 3 else SD - 3 * SLOT
-        as_column = jnp.broadcast_to(meta[t : t + 1, :].astype(F32), (SLOT, SLOT)).T.astype(jnp.int32)
-        length = jnp.broadcast_to(meta[4 + t : 5 + t, :].astype(F32), (SLOT, SLOT)).T.astype(jnp.int32)
+        as_column = jnp.broadcast_to(columns[t : t + 1, :].astype(F32), (SLOT, SLOT)).T.astype(jnp.int32)
+        length = jnp.broadcast_to(lengths[t : t + 1, :].astype(F32), (SLOT, SLOT)).T.astype(jnp.int32)
         inside = (2 * jnp.abs(slots) < length).astype(F32)
         off_x, off_y = (as_column >> 7) - SLOT // 2, (as_column & 127) - SLOT // 2
         squared = off_x * off_x + off_y * off_y + slots * slots
@@ -148,7 +191,7 @@
     turned_trial = jnp.concatenate([masked[0].T, masked[1].T], axis=0)
     high = turned_trial.astype(BF16)
     low = (turned_trial - high.astype(F32)).astype(BF16)
-    loads[0].wait()
+    loads[3].wait()
 
     def z_dot(i):
         return dot(z_out[i], high) + (dot(z_out[i + 1], high) + dot(z_out[i], low))
@@ -176,28 +219,8 @@
             device_id=(b, lax.rem(p + 1, NP)), device_id_type=MESH,
         )
 
-    pl.semaphore_wait(barrier, NP - 1 + NB - 1)
-
-    def share_rows(c, j):
-        return pl.ds(pl.multiple_of((TILES * c + j) * 16, 16), 16)
-
-    def share_copy(c, j, source):
-        return pltpu.make_async_remote_copy(
-            src_ref=orbitals.at[:, :, share_rows(c, j), :], dst_ref=shares.at[source, j],
-            send_sem=share_send.at[c, j], recv_sem=share_recv.at[source, j],
-            device_id=(c, p), device_id_type=MESH,
-        )
-
-    def own_copy(j):
-        return pltpu.make_async_copy(orbitals.at[:, :, share_rows(b, j), :], shares.at[b, j], own_sem.at[j])
-
-    def send_shares(j, carry):
-        for d in range(1, NB):
-            share_copy(lax.rem(b + d, NB), j, b).start()
-        own_copy(j).start()
-        return carry
-
-    send_shares(0, 0)
+
+    pl.semaphore_wait(joined, 7)
 
     def cols_copy(q, source):
         return pltpu.make_async_remote_copy(
@@ -218,8 +241,6 @@
     lax.fori_loop(1, NP, send_tx, 0)
     cols_in[p] = cols_out[...]
     rx[p] = tx[p]
-
-    lax.fori_loop(1, TILES, send_shares, 0)
 
     gram[...] = jnp.zeros_like(gram)
     proj[...] = jnp.zeros_like(proj)
@@ -298,8 +319,8 @@
 
     lax.fori_loop(0, GROUPS, to_window, 0)
 
-    loads[6].wait()
-    loads[8].wait()
+    loads[9].wait()
+    loads[11].wait()
     for t in range(2):
         mask = inside_low[384 + 16 * t : 400 + 16 * t, :]
         for k in range(2):
@@ -323,9 +344,9 @@
 
     gram_step(0)
 
-    for load in loads[2:6]:
+    for load in loads[5:9]:
         load.wait()
-    loads[7].wait()
+    loads[10].wait()
     prod[...] = jnp.zeros_like(prod)
 
     def planes(i, carry):
@@ -400,7 +421,7 @@
 
     all_copies(tx2, rx2, tx2_send, tx2_recv).wait_recv()
 
-    loads[1].wait()
+    loads[4].wait()
     rest_low = rx2[:, 64:80, :].reshape(NP * 16, SLOT).astype(F32)
     for t in range(4):
         first = rx2[:, 16 * t : 16 * t + 16, :].reshape(NP * 16, SLOT)
@@ -576,7 +597,8 @@
 
 def shards(orbitals, trial_bands, potential, stick_column, stick_length):
     pad = (0, 4 * SLOT - SD)
-    meta = jnp.concatenate([jnp.pad(stick_column, pad), jnp.pad(stick_length, pad)]).reshape(8, SLOT)
+    columns = jnp.pad(stick_column, pad).reshape(4, SLOT)
+    lengths = jnp.pad(stick_length, pad).reshape(4, SLOT)
     held = tables()
     any_spec = pl.BlockSpec(memory_space=pl.ANY)
     vmem_spec = pl.BlockSpec(memory_space=pltpu.VMEM)
@@ -588,11 +610,14 @@
             jax.ShapeDtypeStruct(trial_bands.shape, F32),
             jax.ShapeDtypeStruct((REDUCERS, 8, SLOT), F32),
         ),
-        in_specs=[any_spec, vmem_spec, any_spec, vmem_spec] + [any_spec] * len(TABLES),
+        in_specs=[any_spec] * (5 + len(TABLES)),
         out_specs=(any_spec, vmem_spec),
         scratch_shapes=[vmem(held[name].shape, BF16) for name in TABLES]
         + [
             vmem((ZP, GRID, GRID), F32),
+            vmem((2, 1, SD, SLOT), F32),
+            vmem((4, SLOT), jnp.int32),
+            vmem((4, SLOT), jnp.int32),
             vmem((NB, TILES, 2, 32, 16, SLOT), BF16),
             vmem((2, 512, SLOT), F32),
             vmem((8, SLOT), jnp.int32),
@@ -630,7 +655,7 @@
             vmem((REDUCERS, 8, SLOT), F32),
             vmem((NP, 8, SLOT), F32),
             vmem((REDUCERS, 8, SLOT), F32),
-            sem((9,)),
+            sem((12,)),
             sem((NB, TILES)),
             sem((NB, TILES)),
             sem((TILES,)),
@@ -651,11 +676,12 @@
             sem,
             sem((REDUCERS,)),
             sem,
+            pltpu.SemaphoreType.REGULAR,
         ],
         compiler_params=pltpu.CompilerParams(
             collective_id=0, has_side_effects=True, vmem_limit_bytes=62 * 1024 * 1024
         ),
-    )(orbitals, trial_bands, potential, meta, *[jnp.asarray(held[name]) for name in TABLES])
+    )(orbitals, trial_bands, potential, columns, lengths, *[jnp.asarray(held[name]) for name in TABLES])
     applied, intersection, projected = pl.pallas_call(
         finish,
         out_shape=(

time: 108 us -> 106 us (0.981)
  Pallas kernels: 106 us -> 104 us
    pallas_call x1, Pallas kernels: 104 us -> 102 us  [shards(): pl.pallas_call(kernel, out_shape=(jax.ShapeDtypeStruct(trial_bands.shape,...]
    reshape x0 -> x1, local copies, waits for them, and re-layouts: none -> 1.28 us  [shards(): lengths = jnp.pad(stick_length, pad).reshape(4, SLOT)]
where the time goes in v2:
time: 106 us
  Pallas kernels  104 us (98%)
  local copies, waits for them, and re-layouts  1.28 us (1%)
    pallas_call x1, Pallas kernels, shards(): pl.pallas_call(kernel, out_shape=(jax.ShapeDtypeStruct(trial_bands.shape,...  102 us

profile of v2, /device:TPU:1, one launch (start us, length us, event | category | flops | bytes accessed | tf_op | source)
XLA Modules:
  0.0 105.9 jit_solution(17493295507947730388)
XLA Ops:
  0.6 1.3 %pad_bitcast_fusion = (s32[4,128]{1,0:T(4,128)}, s32[4,128]{1,0:T(4,128)}) fusion(s32[416]{0:T(512)} %param.16, s32[416]{0:T(512)} %param.15), kind=kLoop, calls=%fused_computation | loop fusion | bytes 7424 | tf_op jit(solution)/shard_map/reshape | solution.py:601
  1.9 102.2 %shard_map.139 = (f32[2,1,416,128]{3,2,1,0:T(8,128)}, f32[10,8,128]{2,1,0:T(8,128)}) custom-call(bf16[2,32,416,128]{3,2,1,0:T(8,128)(2,1)} %orbitals.1, f32[2,1,416,128]{3,2,1,0:T(8,128)} %trial_h.1, f32[10,320,320]{2,1,0:T(8,128)} %potential.1, s32[4,128]{1,0:T(4,128)} %get-tuple-element.14.columns_h, s32[4,128]{1,0:T(4,128)} %get-tuple-element.13.lengths_h, ...), custom_call_target="tpu_custom_call" | custom-call | tf_op jit(solution)/shard_map/pallas_call | solution.py:607
  104.1 1.8 %shard_map.140 = (f32[2,1,416,128]{3,2,1,0:T(8,128)}, f32[2,32,128]{2,1,0:T(8,128)}, f32[2,4,32]{2,1,0:T(4,128)}) custom-call(f32[2,1,416,128]{3,2,1,0:T(8,128)} %get-tuple-element.8.applied, f32[10,8,128]{2,1,0:T(8,128)} %get-tuple-element.9.final), custom_call_target="tpu_custom_call" | custom-call | tf_op jit(solution)/shard_map/pallas_call | solution.py:685

commit v3 on v2

--- a/solution.py
+++ b/solution.py
@@ -29,7 +29,7 @@
 EXTRA = 8 * SLOT
 GROUP = 4 * SD
 GROUPS = NP // 4
-REDUCERS = 10
+SUMS = 24
 
 
 def split(table):
@@ -82,16 +82,16 @@
 
 
 def kernel(
-    orbitals, trial_h, potential, columns_h, lengths_h, z_out_h, z_back_h, x_out_h, y_out_h, y_back_h, x_back_h, swap_h,
+    orbitals, trial_h, potential, columns, lengths, z_out_h, z_back_h, x_out_h, y_out_h, y_back_h, x_back_h, swap_h,
     applied_out, final_out,
-    z_out, z_back, x_out, y_out, y_back, x_back, swap, pot, trial, columns, lengths,
+    z_out, z_back, x_out, y_out, y_back, x_back, swap, pot, trial,
     shares, masked, cols_out, cols_in, tx, rx, tx2, rx2,
     spots, values, onehot, spread, window, back,
     xin, yin, prod, xback, inside_s, inside_low, kinetic_s, local_s, applied, applied_low, applied_in,
     turned, turned_applied, extra_raw, extra_out, extra_in, gram, proj,
-    part_out, part_in, part_sum, red_in, fin,
+    sum_out, sum_in, row_out, row_in, fin,
     load_sem, share_send, share_recv, own_sem, extra_send, extra_recv, cols_send, cols_recv, tx_send, tx_recv, tx2_send, tx2_recv,
-    app_send, app_recv, part_send, part_recv, red_send, red_recv, fin_send, fin_recv, out_sem, joined,
+    app_send, app_recv, sum_send, sum_recv, row_send, row_recv, fin_send, fin_recv, out_sem, joined,
 ):
     b = lax.axis_index("band")
     p = lax.axis_index("plane")
@@ -115,10 +115,7 @@
         return carry
 
     lax.fori_loop(1, 8, greet, 0)
-    loads = [
-        pltpu.make_async_copy(source, target, load_sem.at[i])
-        for i, (source, target) in enumerate([(columns_h, columns), (lengths_h, lengths), (trial_h, trial)])
-    ]
+    loads = [pltpu.make_async_copy(trial_h, trial, load_sem.at[0])]
     for load in loads:
         load.start()
     pl.semaphore_wait(barrier, 3 + 3 + 7)
@@ -151,7 +148,7 @@
     lax.fori_loop(0, TILES, send_shares, 0)
 
     loads += [
-        pltpu.make_async_copy(source, target, load_sem.at[3 + i])
+        pltpu.make_async_copy(source, target, load_sem.at[1 + i])
         for i, (source, target) in enumerate(
             [
                 (z_out_h, z_out), (z_back_h, z_back), (x_out_h, x_out), (y_out_h, y_out), (y_back_h, y_back),
@@ -160,21 +157,27 @@
             ]
         )
     ]
-    for load in loads[3:]:
+    for load in loads[1:]:
         load.start()
-    for load in loads[:3]:
-        load.wait()
+    loads[0].wait()
 
     shift = 32 * lax.rem(p, 4)
     rest = 384 + pl.multiple_of(shift, 32)
-    cols_out[0:4, :] = columns[...]
+    short = jnp.zeros((1, 4 * SLOT - SD), jnp.int32)
+    column_rows, length_rows = (
+        [held[t * SLOT : (t + 1) * SLOT].reshape(1, SLOT) for t in range(3)]
+        + [jnp.concatenate([held[3 * SLOT : SD].reshape(1, SD - 3 * SLOT), short], axis=1)]
+        for held in (columns, lengths)
+    )
+    for t in range(4):
+        cols_out[t : t + 1, :] = column_rows[t]
     cols_out[4:8, :] = jnp.zeros((4, SLOT), jnp.int32)
     cols_out[3:4, :] = pltpu.roll(cols_out[...], shift, 1)[3:4, :]
     slots = lax.broadcasted_iota(jnp.int32, (SLOT, SLOT), 1) - SLOT // 2
     for t in range(4):
         rows = SLOT if t < 3 else SD - 3 * SLOT
-        as_column = jnp.broadcast_to(columns[t : t + 1, :].astype(F32), (SLOT, SLOT)).T.astype(jnp.int32)
-        length = jnp.broadcast_to(lengths[t : t + 1, :].astype(F32), (SLOT, SLOT)).T.astype(jnp.int32)
+        as_column = jnp.broadcast_to(column_rows[t].astype(F32), (SLOT, SLOT)).T.astype(jnp.int32)
+        length = jnp.broadcast_to(length_rows[t].astype(F32), (SLOT, SLOT)).T.astype(jnp.int32)
         inside = (2 * jnp.abs(slots) < length).astype(F32)
         off_x, off_y = (as_column >> 7) - SLOT // 2, (as_column & 127) - SLOT // 2
         squared = off_x * off_x + off_y * off_y + slots * slots
@@ -191,7 +194,7 @@
     turned_trial = jnp.concatenate([masked[0].T, masked[1].T], axis=0)
     high = turned_trial.astype(BF16)
     low = (turned_trial - high.astype(F32)).astype(BF16)
-    loads[3].wait()
+    loads[1].wait()
 
     def z_dot(i):
         return dot(z_out[i], high) + (dot(z_out[i + 1], high) + dot(z_out[i], low))
@@ -319,8 +322,8 @@
 
     lax.fori_loop(0, GROUPS, to_window, 0)
 
+    loads[7].wait()
     loads[9].wait()
-    loads[11].wait()
     for t in range(2):
         mask = inside_low[384 + 16 * t : 400 + 16 * t, :]
         for k in range(2):
@@ -344,9 +347,9 @@
 
     gram_step(0)
 
-    for load in loads[5:9]:
+    for load in loads[3:7]:
         load.wait()
-    loads[10].wait()
+    loads[8].wait()
     prod[...] = jnp.zeros_like(prod)
 
     def planes(i, carry):
@@ -421,7 +424,7 @@
 
     all_copies(tx2, rx2, tx2_send, tx2_recv).wait_recv()
 
-    loads[4].wait()
+    loads[2].wait()
     rest_low = rx2[:, 64:80, :].reshape(NP * 16, SLOT).astype(F32)
     for t in range(4):
         first = rx2[:, 16 * t : 16 * t + 16, :].reshape(NP * 16, SLOT)
@@ -493,92 +496,72 @@
     imag = gram[0:128, 128:256] - gram[128:256, 0:128]
     proj_real = proj[0:8, 0:128] + proj[8:16, 128:256]
     proj_imag = proj[8:16, 0:128] - proj[0:8, 128:256]
+    both = jnp.concatenate([proj_real[0:NB], proj_imag[0:NB]], axis=0)
     for c in range(NB):
-        part_out[c, 0:32, :] = real[c * 32 : (c + 1) * 32]
-        part_out[c, 32:64, :] = imag[c * 32 : (c + 1) * 32]
-        part_out[c, 64:72, :] = proj_real
-        part_out[c, 72:80, :] = proj_imag
-
-    def part_copy(c, source):
-        return pltpu.make_async_remote_copy(
-            src_ref=part_out.at[c], dst_ref=part_in.at[source], send_sem=part_send.at[c], recv_sem=part_recv.at[source],
-            device_id=(c, p), device_id_type=MESH,
-        )
-
-    for d in range(1, NB):
-        part_copy(lax.rem(b + d, NB), b).start()
-    part_in[b] = part_out[b]
-    for d in range(1, NB):
-        c = lax.rem(b + d, NB)
-        part_copy(c, c).wait_recv()
-    part_sum[...] = ((part_in[0] + part_in[1]) + (part_in[2] + part_in[3])).reshape(REDUCERS, 8, SLOT)
-
-    def red_copy(t):
-        return pltpu.make_async_remote_copy(
-            src_ref=part_sum.at[t], dst_ref=red_in.at[p], send_sem=red_send.at[t], recv_sem=red_recv,
-            device_id=(b, 3 * t), device_id_type=MESH,
-        )
-
-    def fin_copy(t, q):
-        return pltpu.make_async_remote_copy(
-            src_ref=fin.at[t], dst_ref=fin.at[t], send_sem=fin_send, recv_sem=fin_recv.at[t],
-            device_id=(b, q), device_id_type=MESH,
-        )
-
-    mine = p // 3
-    reducer = jnp.logical_and(lax.rem(p, 3) == 0, mine < REDUCERS)
-
-    def send_red(t, carry):
-        @pl.when(3 * t != p)
-        def _():
-            red_copy(t).start()
-
-        return carry
-
-    lax.fori_loop(0, REDUCERS, send_red, 0)
-
-    @pl.when(reducer)
-    def _():
-        red_in[p] = part_sum[mine]
-        all_copies(red_in, red_in, fin_send, red_recv).wait_recv()
-        fin[mine] = jnp.sum(red_in[...], axis=0)
-
-        def send_fin(i, carry):
-            fin_copy(mine, plane_peer(i)).start()
-            return carry
-
-        lax.fori_loop(1, NP, send_fin, 0)
-
-    def wait_fin(t, carry):
-        @pl.when(3 * t != p)
-        def _():
-            fin_copy(t, 3 * t).wait_recv()
-
-        return carry
-
-    lax.fori_loop(0, REDUCERS, wait_fin, 0)
-    final_out[...] = fin[...]
+        for k, part in enumerate((real, imag)):
+            for half in range(2):
+                first = c * 32 + half * 16
+                sum_out[4 * c + 2 * k + half, 0:16, :] = part[first : first + 16]
+                sum_out[4 * c + 2 * k + half, 16:SUMS, :] = both
+    own = 4 * b + row
+
+    def sum_copy(i):
+        to = lax.rem(own + i, 16)
+        return pltpu.make_async_remote_copy(
+            src_ref=sum_out.at[to], dst_ref=sum_in.at[own], send_sem=sum_send, recv_sem=sum_recv,
+            device_id=(to // 4, 8 * lax.rem(to, 4) + seat), device_id_type=MESH,
+        )
+
+    def row_copy(i):
+        return pltpu.make_async_remote_copy(
+            src_ref=row_out, dst_ref=row_in.at[seat], send_sem=row_send, recv_sem=row_recv,
+            device_id=(b, row_peer(i)), device_id_type=MESH,
+        )
+
+    def fin_copy(d):
+        return pltpu.make_async_remote_copy(
+            src_ref=fin.at[row], dst_ref=fin.at[row], send_sem=fin_send, recv_sem=fin_recv,
+            device_id=(b, 8 * lax.rem(row + d, 4) + seat), device_id_type=MESH,
+        )
+
+    def send_sum(i, carry):
+        sum_copy(i).start()
+        return carry
+
+    lax.fori_loop(1, 16, send_sum, 0)
+    sum_in[own] = sum_out[own]
+    sums_there = all_copies(sum_in, sum_in, sum_send, sum_recv, 0, 15)
+    sums_there.wait_recv()
+    row_out[...] = jnp.sum(sum_in[...], axis=0)
+
+    def send_row(i, carry):
+        row_copy(i).start()
+        return carry
+
+    lax.fori_loop(1, 8, send_row, 0)
+    row_in[seat] = row_out[...]
+    rows_there = all_copies(row_in, row_in, row_send, row_recv, 0, 7)
+    rows_there.wait_recv()
+    fin[row] = jnp.sum(row_in[...], axis=0)
+    for d in range(1, 4):
+        fin_copy(d).start()
+    fin_there = all_copies(fin, fin, fin_send, fin_recv, 0, 3)
+    fin_there.wait_recv()
+    for r in range(4):
+        final_out[2 * r] = fin[r, 0:8, :]
+        final_out[2 * r + 1] = fin[r, 8:16, :]
+    final_out[8] = fin[0, 16:SUMS, :]
 
     all_copies(cols_in, cols_in, cols_send, cols_recv).wait_send()
     all_copies(tx, rx, tx_send, tx_recv.at[0]).wait_send()
     all_copies(tx2, rx2, tx2_send, tx2_recv).wait_send()
 
-    @pl.when(reducer)
-    def _():
-        all_copies(red_in, red_in, fin_send, red_recv).wait_send()
-
-    def red_sent(t, carry):
-        @pl.when(3 * t != p)
-        def _():
-            red_copy(t).wait_send()
-
-        return carry
-
-    lax.fori_loop(0, REDUCERS, red_sent, 0)
+    sums_there.wait_send()
+    rows_there.wait_send()
+    fin_there.wait_send()
     for d in range(1, NB):
         c = lax.rem(b + d, NB)
         extra_copy(c, b).wait_send()
-        part_copy(c, b).wait_send()
         for j in range(TILES):
             share_copy(c, j, b).wait_send()
         for j in range(TILES + 1):
@@ -592,13 +575,10 @@
     for k in range(2):
         for r in range(4):
             intersection[k, 8 * r : 8 * r + 8, :] = final[4 * k + r]
-        projected[k] = pltpu.roll(final[8 + k], shift, 1)[0:NB, 0:32]
+        projected[k] = pltpu.roll(final[8], shift, 1)[NB * k : NB * k + NB, 0:32]
 
 
 def shards(orbitals, trial_bands, potential, stick_column, stick_length):
-    pad = (0, 4 * SLOT - SD)
-    columns = jnp.pad(stick_column, pad).reshape(4, SLOT)
-    lengths = jnp.pad(stick_length, pad).reshape(4, SLOT)
     held = tables()
     any_spec = pl.BlockSpec(memory_space=pl.ANY)
     vmem_spec = pl.BlockSpec(memory_space=pltpu.VMEM)
@@ -608,16 +588,14 @@
         kernel,
         out_shape=(
             jax.ShapeDtypeStruct(trial_bands.shape, F32),
-            jax.ShapeDtypeStruct((REDUCERS, 8, SLOT), F32),
+            jax.ShapeDtypeStruct((9, 8, SLOT), F32),
         ),
-        in_specs=[any_spec] * (5 + len(TABLES)),
+        in_specs=[any_spec] * 3 + [vmem_spec] * 2 + [any_spec] * len(TABLES),
         out_specs=(any_spec, vmem_spec),
         scratch_shapes=[vmem(held[name].shape, BF16) for name in TABLES]
         + [
             vmem((ZP, GRID, GRID), F32),
             vmem((2, 1, SD, SLOT), F32),
-            vmem((4, SLOT), jnp.int32),
-            vmem((4, SLOT), jnp.int32),
             vmem((NB, TILES, 2, 32, 16, SLOT), BF16),
             vmem((2, 512, SLOT), F32),
             vmem((8, SLOT), jnp.int32),
@@ -650,12 +628,12 @@
             vmem((NB, 2, 32, EXTRA), BF16),
             vmem((256, 256), F32),
             vmem((16, 256), F32),
-            vmem((NB, 80, SLOT), F32),
-            vmem((NB, 80, SLOT), F32),
-            vmem((REDUCERS, 8, SLOT), F32),
-            vmem((NP, 8, SLOT), F32),
-            vmem((REDUCERS, 8, SLOT), F32),
-            sem((12,)),
+            vmem((16, SUMS, SLOT), F32),
+            vmem((16, SUMS, SLOT), F32),
+            vmem((SUMS, SLOT), F32),
+            vmem((8, SUMS, SLOT), F32),
+            vmem((4, SUMS, SLOT), F32),
+            sem((10,)),
             sem((NB, TILES)),
             sem((NB, TILES)),
             sem((TILES,)),
@@ -669,19 +647,19 @@
             sem,
             sem((NB, TILES + 1)),
             sem((NB, TILES + 1)),
-            sem((NB,)),
-            sem((NB,)),
-            sem((REDUCERS,)),
-            sem,
-            sem,
-            sem((REDUCERS,)),
+            sem,
+            sem,
+            sem,
+            sem,
+            sem,
+            sem,
             sem,
             pltpu.SemaphoreType.REGULAR,
         ],
         compiler_params=pltpu.CompilerParams(
             collective_id=0, has_side_effects=True, vmem_limit_bytes=62 * 1024 * 1024
         ),
-    )(orbitals, trial_bands, potential, columns, lengths, *[jnp.asarray(held[name]) for name in TABLES])
+    )(orbitals, trial_bands, potential, stick_column, stick_length, *[jnp.asarray(held[name]) for name in TABLES])
     applied, intersection, projected = pl.pallas_call(
         finish,
         out_shape=(

time: 106 us -> 104 us (0.981)
  local copies, waits for them, and re-layouts: 1.28 us -> 0 us
    reshape x1 -> x0, local copies, waits for them, and re-layouts: 1.28 us -> none  [shards(): lengths = jnp.pad(stick_length, pad).reshape(4, SLOT)]
where the time goes in v3:
time: 104 us
  Pallas kernels  103 us (99%)
    pallas_call x1, Pallas kernels, shards(): pl.pallas_call(kernel, out_shape=(jax.ShapeDtypeStruct(trial_bands.shape,...  101 us

profile of v3, /device:TPU:1, one launch (start us, length us, event | category | flops | bytes accessed | tf_op | source)
XLA Modules:
  0.0 103.7 jit_solution(11836420037504942326)
XLA Ops:
  0.6 101.3 %shard_map.139 = (f32[2,1,416,128]{3,2,1,0:T(8,128)}, f32[9,8,128]{2,1,0:T(8,128)}) custom-call(bf16[2,32,416,128]{3,2,1,0:T(8,128)(2,1)} %orbitals.1, f32[2,1,416,128]{3,2,1,0:T(8,128)} %trial_h.1, f32[10,320,320]{2,1,0:T(8,128)} %potential.1, s32[416]{0:T(512)} %columns.1, s32[416]{0:T(512)} %lengths.1, bf16[4,512,256]{2,1,0:T(8,128)(2,1)} %constant.14.clone.z_out_h, ...), custom_call_target="tpu_custom_call" | custom-call | tf_op jit(solution)/shard_map/pallas_call | solution.py:587
  101.9 1.8 %shard_map.140 = (f32[2,1,416,128]{3,2,1,0:T(8,128)}, f32[2,32,128]{2,1,0:T(8,128)}, f32[2,4,32]{2,1,0:T(4,128)}) custom-call(f32[2,1,416,128]{3,2,1,0:T(8,128)} %get-tuple-element.8.applied, f32[9,8,128]{2,1,0:T(8,128)} %get-tuple-element.9.final), custom_call_target="tpu_custom_call" | custom-call | tf_op jit(solution)/shard_map/pallas_call | solution.py:663
